TPU v7x, 128 devices: a whole 4x4x4 slice. The times are simulated.
128 devices in a mesh: ctx: 16 (over x_hi, z, core), tp: 8 (over y, x_lo).
Axes of the slice: x: 4 (x_hi: 2, x_lo: 2; x = x_hi * 2 + x_lo), y: 4, z: 4, core: 2. Of those that a mesh axis runs over, the one named last changes fastest.
Arguments:
- queries: bfloat16 [4, 128, 128, 128], P(None, ('ctx', 'tp')), may hold values from -6.5 to 6.5
- new_keys: bfloat16 [4, 128, 8, 128], P(None, ('ctx', 'tp')), may hold values from -4 to 4
- turn_value_rows: bfloat16 [4, 128, 8, 128], P(None, ('ctx', 'tp')), may hold values from -4 to 4
- cache_keys: bfloat16 [4, 32768, 8, 128], P(None, 'ctx', 'tp'), may hold values from -4 to 4
- cache_values: bfloat16 [4, 32768, 8, 128], P(None, 'ctx', 'tp'), may hold values from -4 to 4
- cached_len: int32 [4], replicated, may hold values from 1 to 32768, 81920 in all
- new_len: int32 [4], replicated, may hold values from 1 to 128, as said below
- fold: int32 [16], replicated, may hold values from 0 to 15, each once
Outputs:
- attended: bfloat16 [4, 128, 128, 128], P(None, ('ctx', 'tp'))
Inputs may be any that keep to these rules, and one draw needn't show every extreme that they name: `cached_len`: one rollout has a full cache. `new_len`: one rollout fills all 128 slots. `fold`: a permutation of the storage blocks.
All inputs are finite; a program needn't handle non-finite values.
Results may differ from a plain program's by a relative error of at most 0.025.
Values may be sent and summed in bfloat16 or wider, within the bound.
A program may use at most 128 MiB of HBM per device.

v0:
```python
import functools

import jax
import jax.numpy as jnp
from jax import lax
from jax.experimental import pallas as pl
from jax.experimental.pallas import tpu as pltpu
from jax.sharding import PartitionSpec as P

MESH = pl.DeviceIdType.MESH
BF16 = jnp.bfloat16
F32 = jnp.float32
LOG2E = 1.4426950408889634
CLOSED = -1e30
ROWS = 128
TAIL = 16
CHUNK = 512
TILES = ((0, 1), (3, 4), (2, 5), (6, 7))
GREETED = (2, 6, 8, 4, 10, 14, 12, 1)
ORDER = ((0, 0), (0, 1), (1, 0), (1, 1), (0, 2), (0, 3), (1, 2), (1, 3),
         (2, 3), (2, 2), (2, 1), (2, 0), (3, 3), (3, 2), (3, 1), (3, 0))


def flipped(index, mask, bits):
    result = 0
    for k in range(bits):
        bit = lax.rem(lax.div(index, 1 << k), 2)
        result = result + ((1 - bit) if (mask >> k) & 1 else bit) * (1 << k)
    return result


def contract(a, b, ca, cb):
    return lax.dot_general(a, b, (((ca,), (cb,)), ((), ())), preferred_element_type=F32)


def await_bytes(ref, sem):
    pltpu.make_async_copy(ref, ref, sem).wait()


def kernel(
    q_hbm, nk_hbm, nv_hbm, k_hbm, v_hbm, clen_hbm, nlen_hbm, fold_hbm, out_ref,
    qall, kbuf, vaug, s0, s1, m0, m1, oloc, r1, cp, r2, fin, onew, lnew,
    nk_ref, nv_ref, stage_f, stage, kva, asm, kvg, clen_ref, nlen_ref, fold_ref,
    k_sem, v_sem, own_sem, small_sem, a_send, a_recv, kv_send, kv_recv, b_send, b_recv, g_send, g_recv,
    r1_send, r1_recv, r2_send, r2_recv, r3_send, r3_recv, r3_own,
):
    c = lax.axis_index("ctx")
    t = lax.axis_index("tp")
    rollouts = k_hbm.shape[0]
    span = k_hbm.shape[1]
    slots = qall.shape[1]
    tps = stage.shape[0]
    group = ROWS // tps
    scale = 128 ** -0.5 * LOG2E
    ctx_peer = [flipped(c, j, 4) for j in range(slots)]
    tp_peer = [flipped(t, i, 3) for i in range(tps)]
    partner = ctx_peer[1]
    my_rows = pl.ds(pl.multiple_of(t * group, group), group)

    def rows_of(i):
        return pl.ds(pl.multiple_of(tp_peer[i] * group, group), group)

    def remote(src, dst, send, recv, ctx, tp):
        pltpu.make_async_remote_copy(
            src_ref=src, dst_ref=dst, send_sem=send, recv_sem=recv,
            device_id=(ctx, tp), device_id_type=MESH,
        ).start()

    barrier = pltpu.get_barrier_semaphore()
    for i in range(1, tps):
        pl.semaphore_signal(barrier, inc=1, device_id=(c, tp_peer[i]), device_id_type=MESH)
    for j in GREETED:
        pl.semaphore_signal(barrier, inc=1, device_id=(ctx_peer[j], t), device_id_type=MESH)

    small = [
        pltpu.make_async_copy(src, dst, small_sem.at[i])
        for i, (src, dst) in enumerate((
            (nk_hbm, nk_ref), (nv_hbm, nv_ref), (clen_hbm, clen_ref), (nlen_hbm, nlen_ref), (fold_hbm, fold_ref)))
    ]
    for copy in small:
        copy.start()
    own_copy = pltpu.make_async_copy(q_hbm.at[:, my_rows, :], qall.at[:, 0, my_rows, :], own_sem)
    own_copy.start()
    k_copies, v_copies = [], []
    for b in range(rollouts):
        k_copies.append(pltpu.make_async_copy(k_hbm.at[b], kbuf.at[b], k_sem.at[b]))
        v_copies.append(pltpu.make_async_copy(v_hbm.at[b], vaug.at[b, :, pl.ds(0, 128)], v_sem.at[b]))
        k_copies[b].start()
        v_copies[b].start()

    for copy in small:
        copy.wait()
    stage_f[...] = jnp.zeros_like(stage_f)
    for b in range(rollouts):
        keys_f = nk_ref[b].astype(F32)
        vals_f = nv_ref[b].astype(F32)
        for i in range(tps):
            stage_f[i, b : b + 1, :] = keys_f[i : i + 1, :]
            stage_f[i, rollouts + b : rollouts + b + 1, :] = vals_f[i : i + 1, :]
    stage[...] = stage_f[...].astype(BF16)
    kva[pl.ds(t, 1)] = stage[pl.ds(t, 1)]

    pl.semaphore_wait(barrier, tps - 1 + len(GREETED))

    def send_a(b):
        for i in range(1, tps):
            remote(q_hbm.at[b, rows_of(i), :], qall.at[b, 0, my_rows, :],
                   a_send.at[b], a_recv.at[b], c, tp_peer[i])

    def wait_a(b):
        await_bytes(qall.at[b, 0, pl.ds(0, ROWS - group), :], a_recv.at[b])

    for b in range(rollouts):
        send_a(b)
    for i in range(1, tps):
        remote(stage.at[tp_peer[i]], kva.at[t], kv_send, kv_recv, c, tp_peer[i])

    def send_b(b):
        for j in GREETED:
            remote(qall.at[b, 0], qall.at[b, j], b_send.at[b], b_recv.at[b, j], ctx_peer[j], t)

    def pass_on(b, q):
        for p in TILES[q]:
            if p:
                await_bytes(qall.at[b, 2 * p], b_recv.at[b, 2 * p])
                remote(qall.at[b, 2 * p], qall.at[b, 2 * p + 1], b_send.at[b], b_recv.at[b, 2 * p + 1], partner, t)

    def wait_odd(b, q):
        for p in TILES[q]:
            await_bytes(qall.at[b, 2 * p + 1], b_recv.at[b, 2 * p + 1])

    def kv_pass_on():
        for j in range(2, slots, 2):
            await_bytes(kvg.at[j], g_recv.at[j])
            remote(kvg.at[j], kvg.at[j + 1], g_send, g_recv.at[j + 1], partner, t)

    def prepare(b):
        open_count = clen_ref[b] - fold_ref[c] * span
        for r in range(0, span, 256):
            row = lax.broadcasted_iota(jnp.int32, (256, 128), 0) + r
            is_open = row < open_count
            first = kbuf[b, 0:16, :].astype(F32)[0:1, :]
            kbuf[b, r : r + 256, :] = jnp.where(
                is_open, kbuf[b, r : r + 256, :].astype(F32), first).astype(BF16)
            vaug[b, r : r + 256, 0:128] = jnp.where(
                is_open, vaug[b, r : r + 256, 0:128].astype(F32), 0.0).astype(BF16)
            vaug[b, r : r + 256, 128:256] = jnp.where(is_open, 1.0, 0.0).astype(BF16)

    eye = (lax.broadcasted_iota(jnp.int32, (ROWS, ROWS), 0)
           == lax.broadcasted_iota(jnp.int32, (ROWS, ROWS), 1))

    def tile_queries(b, q):
        return jnp.concatenate([qall[b, 2 * p : 2 * p + 2] for p in TILES[q]], axis=0)

    def score_tile(b, queries, s_ref, m_ref):
        queries = queries.reshape(4 * ROWS, 128)
        top = None
        for k in range(0, span, CHUNK):
            s = contract(queries, kbuf[b, k : k + CHUNK, :], 1, 1)
            s_ref[:, k : k + CHUNK] = s
            for x in range(0, CHUNK, 128):
                part = s[:, x : x + 128]
                top = part if top is None else jnp.maximum(top, part)
        m_ref[...] = jnp.broadcast_to(jnp.max(top, axis=1, keepdims=True) * scale, m_ref.shape)

    def stat_rows(stat):
        high = stat.astype(BF16).astype(F32)
        middle = (stat - high).astype(BF16).astype(F32)
        low = stat - high - middle
        row = lax.broadcasted_iota(jnp.int32, (TAIL, 128), 0)
        return jnp.where(row == 0, high, jnp.where(row == 1, middle, jnp.where(row == 2, low, 0.0))).astype(BF16)

    def stat_of(rows):
        return jnp.sum(rows.astype(F32), axis=0, keepdims=True)

    def diagonal(weight):
        return jnp.where(eye, jnp.broadcast_to(weight, (ROWS, ROWS)), 0.0).astype(BF16)

    def to_row(replicated):
        return jnp.sum(jnp.where(eye, replicated, 0.0), axis=0, keepdims=True)

    def finish(total, weight, top):
        live = weight > 0.0
        safe = jnp.where(live, weight, 1.0)
        return (jnp.where(live, total / safe, 0.0), jnp.where(live, top + jnp.log2(safe), CLOSED))

    def weigh_tile(b, q, s_ref, m_ref):
        top = m_ref[...]
        total = None
        for k in range(0, span, CHUNK):
            parts = []
            for x in range(k, k + CHUNK, 128):
                parts.append(jnp.exp2(s_ref[:, x : x + 128] * scale - top).astype(BF16))
            d = contract(jnp.concatenate(parts, axis=1), vaug[b, k : k + CHUNK, :], 1, 0)
            total = d if total is None else total + d
        mean, level = finish(total[:, 0:128], total[:, 128:256], top)
        mean = mean.astype(BF16)
        for g in range(4):
            rows = slice(g * ROWS, (g + 1) * ROWS)
            oloc[b, q, g // 2, g % 2, 0:ROWS, :] = mean[rows]
            oloc[b, q, g // 2, g % 2, ROWS : ROWS + TAIL, :] = stat_rows(to_row(level[rows]))

    def blend(pieces, levels):
        top = functools.reduce(jnp.maximum, levels)
        weights = [jnp.exp2(level - top) for level in levels]
        total = functools.reduce(jnp.add, weights)
        share = 1.0 / total
        left = jnp.concatenate([diagonal(weight * share) for weight in weights], axis=1)
        mixed = contract(left, jnp.concatenate(pieces, axis=0), 1, 0)
        return mixed, top + jnp.log2(total)

    def chip_blend(b, q):
        for g, pair in enumerate(TILES[q]):
            mixed, level = blend(
                [oloc[b, q, g, 0, 0:ROWS, :], r1[b, q, g, 0:ROWS, :]],
                [stat_of(oloc[b, q, g, 0, ROWS : ROWS + TAIL, :]), stat_of(r1[b, q, g, ROWS : ROWS + TAIL, :])],
            )
            cp[b, pair, 0:ROWS, :] = mixed.astype(BF16)
            cp[b, pair, ROWS : ROWS + TAIL, :] = stat_rows(level)

    def new_part(b):
        blocks = [kvg[j, b].astype(F32) for j in range(slots)]
        keys = jnp.concatenate([x[0:8] for x in blocks], axis=0).astype(BF16)
        values = jnp.concatenate([x[8:16] for x in blocks], axis=0).astype(BF16)
        column = lax.broadcasted_iota(jnp.int32, (ROWS, ROWS), 1)
        position = lax.rem(column, tps)
        for j in range(slots):
            position = position + jnp.where(lax.div(column, tps) == j, ctx_peer[j] * tps, 0)
        row = lax.broadcasted_iota(jnp.int32, (ROWS, ROWS), 0)
        allowed = position <= c * tps + lax.div(row, group)
        s = jnp.where(allowed, contract(qall[b, 0, 0:ROWS, :], keys, 1, 1) * scale, CLOSED)
        top = jnp.max(s, axis=1, keepdims=True)
        p = jnp.exp2(s - top)
        weight = jnp.sum(p, axis=1, keepdims=True)
        mean = contract(p.astype(BF16), values, 1, 0) / weight
        onew[b] = mean.astype(BF16)
        lnew[b] = jnp.broadcast_to(
            to_row(jnp.broadcast_to(top + jnp.log2(weight), (ROWS, ROWS))), (8, 128))

    def last_blend(b):
        sources = [cp.at[b, 0]] + [r2.at[b, p] for p in range(1, slots // 2)]
        pieces = [x[0:ROWS, :] for x in sources] + [onew[b]]
        levels = [stat_of(x[ROWS : ROWS + TAIL, :]) for x in sources] + [lnew[b, 0:1, :]]
        mixed, _ = blend(pieces, levels)
        token = c * tps + lax.div(lax.broadcasted_iota(jnp.int32, (ROWS, 128), 0), group)
        fin[b] = jnp.where(token < nlen_ref[b], mixed, 0.0).astype(BF16)

    def send_r1(b, q):
        remote(oloc.at[b, q, :, 1], r1.at[b, q], r1_send.at[b], r1_recv.at[b, q], partner, t)

    def wait_r1(b, q):
        await_bytes(r1.at[b, q], r1_recv.at[b, q])

    def send_r2(b, q):
        for p in TILES[q]:
            if p:
                remote(cp.at[b, p], r2.at[b, p], r2_send.at[b], r2_recv.at[b], ctx_peer[2 * p], t)

    def wait_r2(b):
        await_bytes(r2.at[b, pl.ds(1, slots // 2 - 1)], r2_recv.at[b])

    def send_r3(b):
        for i in range(1, tps):
            remote(fin.at[b, rows_of(i), :], out_ref.at[b, my_rows, :], r3_send, r3_recv, c, tp_peer[i])

    for b in range(rollouts):
        k_copies[b].wait()
        v_copies[b].wait()
        prepare(b)
    own_copy.wait()
    wait_a(0)
    send_b(0)
    wait_a(1)
    send_b(1)
    pass_on(0, 0)
    pass_on(0, 1)
    wait_odd(0, 0)
    bufs = ((s0, m0), (s1, m1))
    score_tile(0, tile_queries(0, 0), *bufs[0])

    def kv_start():
        await_bytes(kva.at[pl.ds(0, tps - 1)], kv_recv)
        for i in range(tps):
            block = kva[i].astype(F32)
            for b in range(rollouts):
                asm[b, i : i + 1, :] = block[b : b + 1, :]
                asm[b, tps + i : tps + i + 1, :] = block[rollouts + b : rollouts + b + 1, :]
        kvg[0] = asm[...].astype(BF16)
        for j in GREETED:
            remote(kvg.at[0], kvg.at[j], g_send, g_recv.at[j], ctx_peer[j], t)

    def kv_end():
        for j in range(1, slots, 2):
            await_bytes(kvg.at[j], g_recv.at[j])

    def begin(b):
        wait_a(b)
        send_b(b)

    def finish_rollout(b):
        last_blend(b)
        send_r3(b)

    count = len(ORDER)
    before, beside, after = ({n: [] for n in range(count + 2)} for _ in range(3))

    def at(when, step, what, *args):
        when[step].append((what, args))

    at(before, 0, begin, 2)
    at(before, 1, kv_start)
    at(before, 3, begin, 3)
    at(before, 7, kv_pass_on)
    at(before, 9, kv_end)
    for n, (b, q) in enumerate(ORDER):
        if n >= 2:
            at(before, n - 2, pass_on, b, q)
    for n, (b, q) in enumerate(ORDER):
        if n >= 1:
            at(before, n - 1, wait_odd, b, q)
        at(after, n, send_r1, b, q)
        at(before, n + 2, wait_r1, b, q)
        at(beside, n + 2, chip_blend, b, q)
        at(after, n + 2, send_r2, b, q)
    for b in range(rollouts):
        at(beside, 9 + b, new_part, b)
    for b, step in ((0, 12), (1, 14)):
        at(before, step, wait_r2, b)
        at(beside, step, last_blend, b)
        at(after, step, send_r3, b)

    for n, (b, q) in enumerate(ORDER):
        for what, args in before[n]:
            what(*args)
        if n + 1 < len(ORDER):
            nb, nq = ORDER[n + 1]
            score_tile(nb, tile_queries(nb, nq), *bufs[(n + 1) % 2])
        weigh_tile(b, q, *bufs[n % 2])
        for what, args in beside[n] + after[n]:
            what(*args)
    for end in (count, count + 1):
        for what, args in before[end] + beside[end] + after[end]:
            what(*args)
    for b in (2, 3):
        wait_r2(b)
        finish_rollout(b)
    keep = pltpu.make_async_copy(fin.at[:, my_rows, :], out_ref.at[:, my_rows, :], r3_own)
    keep.start()

    for b in range(rollouts):
        await_bytes(qall.at[b, 0, pl.ds(0, ROWS - group), :], a_send.at[b])
        await_bytes(qall.at[b, pl.ds(0, slots - 1)], b_send.at[b])
        await_bytes(r1.at[b], r1_send.at[b])
        await_bytes(r2.at[b, pl.ds(1, slots // 2 - 1)], r2_send.at[b])
    await_bytes(kva.at[pl.ds(0, tps - 1)], kv_send)
    await_bytes(kvg.at[pl.ds(0, slots - 1)], g_send)
    await_bytes(fin.at[:, pl.ds(0, ROWS - group), :], r3_send)
    await_bytes(fin.at[:, pl.ds(0, ROWS - group), :], r3_recv)
    keep.wait()


def shards(queries, new_keys, turn_value_rows, cache_keys, cache_values, cached_len, new_len, fold):
    rollouts, span = cache_keys.shape[0], cache_keys.shape[1]
    slots, tps = lax.axis_size("ctx"), lax.axis_size("tp")
    tiles = slots // 4
    any_space = pl.BlockSpec(memory_space=pl.ANY)
    dma = pltpu.SemaphoreType.DMA
    block = (ROWS + TAIL, 128)
    out = pl.pallas_call(
        kernel,
        out_shape=jax.ShapeDtypeStruct((rollouts, 128, 128), BF16),
        in_specs=[any_space] * 8,
        out_specs=any_space,
        scratch_shapes=[
            pltpu.VMEM((rollouts, slots, ROWS, 128), BF16),
            pltpu.VMEM((rollouts, span, 128), BF16),
            pltpu.VMEM((rollouts, span, 256), BF16),
            pltpu.VMEM((4 * ROWS, span), F32),
            pltpu.VMEM((4 * ROWS, span), F32),
            pltpu.VMEM((4 * ROWS, 128), F32),
            pltpu.VMEM((4 * ROWS, 128), F32),
            pltpu.VMEM((rollouts, tiles, 2, 2) + block, BF16),
            pltpu.VMEM((rollouts, tiles, 2) + block, BF16),
            pltpu.VMEM((rollouts, slots // 2) + block, BF16),
            pltpu.VMEM((rollouts, slots // 2) + block, BF16),
            pltpu.VMEM((rollouts, ROWS, 128), BF16),
            pltpu.VMEM((rollouts, ROWS, 128), BF16),
            pltpu.VMEM((rollouts, 8, 128), F32),
            pltpu.VMEM((rollouts, tps, 128), BF16),
            pltpu.VMEM((rollouts, tps, 128), BF16),
            pltpu.VMEM((tps, TAIL, 128), F32),
            pltpu.VMEM((tps, TAIL, 128), BF16),
            pltpu.VMEM((tps, TAIL, 128), BF16),
            pltpu.VMEM((rollouts, TAIL, 128), F32),
            pltpu.VMEM((slots, rollouts, TAIL, 128), BF16),
            pltpu.SMEM((rollouts,), jnp.int32), pltpu.SMEM((rollouts,), jnp.int32),
            pltpu.SMEM((slots,), jnp.int32),
            dma((rollouts,)), dma((rollouts,)), dma, dma((5,)),
            dma((rollouts,)), dma((rollouts,)),
            dma, dma,
            dma((rollouts,)), dma((rollouts, slots)),
            dma, dma((slots,)),
            dma((rollouts,)), dma((rollouts, tiles)),
            dma((rollouts,)), dma((rollouts,)),
            dma, dma, dma,
        ],
        compiler_params=pltpu.CompilerParams(
            collective_id=0, has_side_effects=True, vmem_limit_bytes=56 << 20),
        name="turn_attention",
    )(
        queries[:, 0], new_keys[:, 0], turn_value_rows[:, 0],
        cache_keys[:, :, 0], cache_values[:, :, 0], cached_len, new_len, fold,
    )
    return out[:, None]


def solution(mesh):
    in_specs = (
        P(None, ("ctx", "tp"), None, None),
        P(None, ("ctx", "tp"), None, None),
        P(None, ("ctx", "tp"), None, None),
        P(None, "ctx", "tp", None),
        P(None, "ctx", "tp", None),
        P(),
        P(),
        P(),
    )
    out_specs = P(None, ("ctx", "tp"), None, None)
    return jax.shard_map(shards, mesh=mesh, in_specs=in_specs, out_specs=out_specs, check_vma=False)
```

profile of v0, /device:TPU:0, one launch (start us, length us, event | category | flops | bytes accessed | tf_op | source)
XLA Modules:
  0.0 60.9 jit_solution(15167414446213635085)
XLA Ops:
  0.0 59.3 %turn_attention.1 = bf16[4,128,128]{2,1,0:T(8,128)(2,1)} custom-call(bf16[4,128,128]{2,1,0:T(8,128)(2,1)} %bitcast.11, bf16[4,8,128]{2,1,0:T(8,128)(2,1)} %bitcast.12, bf16[4,8,128]{2,1,0:T(8,128)(2,1)} %bitcast.13, bf16[4,2048,128]{2,1,0:T(8,128)(2,1)} %bitcast.8, bf16[4,2048,128]{2,1,0:T(8,128)(2,1)} %bitcast.9, s32[4]{0:T(128)} %clen_hbm.1, s32[4]{0:T(128)} %nlen_hbm.1, ...), custom_call_target="tpu_custom_call" | custom-call | tf_op jit(solution)/shard_map/turn_attention/pallas_call | solution.py:369
  59.3 1.6 %copy.11 = bf16[4,1,128,128]{3,2,1,0:T(8,128)(2,1)} copy(bf16[4,1,128,128]{3,2,1,0:T(8,128)(2,1)} %bitcast.10) | data formatting | bytes 262144
where the time goes:
time: 61.2 us; the launch traced here: 60.9 us
  Pallas kernels  59.3 us (97%)
  local copies, waits for them, and re-layouts  1.57 us (3%)
    pallas_call x1, Pallas kernels, shards(): pl.pallas_call(kernel, out_shape=jax.ShapeDtypeStruct((rollouts, 128, 128...  59.3 us
    unnamed x1, local copies, waits for them, and re-layouts  1.57 us

commit v1 on v0

--- a/solution.py
+++ b/solution.py
@@ -15,10 +15,17 @@
 ROWS = 128
 TAIL = 16
 CHUNK = 512
-TILES = ((0, 1), (3, 4), (2, 5), (6, 7))
-GREETED = (2, 6, 8, 4, 10, 14, 12, 1)
-ORDER = ((0, 0), (0, 1), (1, 0), (1, 1), (0, 2), (0, 3), (1, 2), (1, 3),
-         (2, 3), (2, 2), (2, 1), (2, 0), (3, 3), (3, 2), (3, 1), (3, 0))
+NEAR = (2, 6, 8, 4)
+FAR = (10, 14, 12)
+LAST = (3, 1)
+GREETED = NEAR + FAR + (1,) + tuple(2 * p + 1 for p in LAST)
+ORDER = (
+    ((0, 0), (1, 0)), ((2, 0), (3, 0)),
+    ((0, 1), (0, 3)), ((0, 4), (0, 2)), ((0, 5), (0, 6)), ((0, 7), (1, 1)),
+    ((1, 3), (1, 4)), ((1, 2), (1, 5)), ((1, 6), (1, 7)),
+    ((2, 7), (2, 6)), ((2, 5), (2, 2)), ((2, 4), (2, 3)), ((2, 1), (3, 7)),
+    ((3, 6), (3, 5)), ((3, 2), (3, 4)), ((3, 3), (3, 1)),
+)
 
 
 def flipped(index, mask, bits):
@@ -39,10 +46,10 @@
 
 def kernel(
     q_hbm, nk_hbm, nv_hbm, k_hbm, v_hbm, clen_hbm, nlen_hbm, fold_hbm, out_ref,
-    qall, kbuf, vaug, s0, s1, m0, m1, oloc, r1, cp, r2, fin, onew, lnew,
+    qall, kbuf, vaug, s0, s1, m0, m1, oloc, r1, cp, r2, rx, fin, onew, lnew,
     nk_ref, nv_ref, stage_f, stage, kva, asm, kvg, clen_ref, nlen_ref, fold_ref,
     k_sem, v_sem, own_sem, small_sem, a_send, a_recv, kv_send, kv_recv, b_send, b_recv, g_send, g_recv,
-    r1_send, r1_recv, r2_send, r2_recv, r3_send, r3_recv, r3_own,
+    r1_send, r1_recv, r2_send, r2_recv, rx_send, rx_recv, r3_send, r3_recv, r3_own,
 ):
     c = lax.axis_index("ctx")
     t = lax.axis_index("tp")
@@ -115,18 +122,17 @@
     for i in range(1, tps):
         remote(stage.at[tp_peer[i]], kva.at[t], kv_send, kv_recv, c, tp_peer[i])
 
-    def send_b(b):
-        for j in GREETED:
+    def send_b(b, *to):
+        for j in to:
             remote(qall.at[b, 0], qall.at[b, j], b_send.at[b], b_recv.at[b, j], ctx_peer[j], t)
 
-    def pass_on(b, q):
-        for p in TILES[q]:
-            if p:
-                await_bytes(qall.at[b, 2 * p], b_recv.at[b, 2 * p])
-                remote(qall.at[b, 2 * p], qall.at[b, 2 * p + 1], b_send.at[b], b_recv.at[b, 2 * p + 1], partner, t)
-
-    def wait_odd(b, q):
-        for p in TILES[q]:
+    def pass_on(*pairs):
+        for b, p in pairs:
+            await_bytes(qall.at[b, 2 * p], b_recv.at[b, 2 * p])
+            remote(qall.at[b, 2 * p], qall.at[b, 2 * p + 1], b_send.at[b], b_recv.at[b, 2 * p + 1], partner, t)
+
+    def wait_odd(*pairs):
+        for b, p in pairs:
             await_bytes(qall.at[b, 2 * p + 1], b_recv.at[b, 2 * p + 1])
 
     def kv_pass_on():
@@ -149,19 +155,23 @@
     eye = (lax.broadcasted_iota(jnp.int32, (ROWS, ROWS), 0)
            == lax.broadcasted_iota(jnp.int32, (ROWS, ROWS), 1))
 
-    def tile_queries(b, q):
-        return jnp.concatenate([qall[b, 2 * p : 2 * p + 2] for p in TILES[q]], axis=0)
-
-    def score_tile(b, queries, s_ref, m_ref):
-        queries = queries.reshape(4 * ROWS, 128)
-        top = None
-        for k in range(0, span, CHUNK):
-            s = contract(queries, kbuf[b, k : k + CHUNK, :], 1, 1)
-            s_ref[:, k : k + CHUNK] = s
-            for x in range(0, CHUNK, 128):
-                part = s[:, x : x + 128]
-                top = part if top is None else jnp.maximum(top, part)
-        m_ref[...] = jnp.broadcast_to(jnp.max(top, axis=1, keepdims=True) * scale, m_ref.shape)
+    def by_rollout(pairs):
+        if pairs[0][0] == pairs[1][0]:
+            return [(pairs[0][0], [p for _, p in pairs], slice(0, 4 * ROWS))]
+        return [(b, [p], slice(2 * ROWS * i, 2 * ROWS * (i + 1))) for i, (b, p) in enumerate(pairs)]
+
+    def score_step(pairs, s_ref, m_ref):
+        for b, members, rows in by_rollout(pairs):
+            queries = jnp.concatenate([qall[b, 2 * p : 2 * p + 2] for p in members], axis=0)
+            queries = queries.reshape(2 * ROWS * len(members), 128)
+            top = None
+            for k in range(0, span, CHUNK):
+                s = contract(queries, kbuf[b, k : k + CHUNK, :], 1, 1)
+                s_ref[rows, k : k + CHUNK] = s
+                for x in range(0, CHUNK, 128):
+                    part = s[:, x : x + 128]
+                    top = part if top is None else jnp.maximum(top, part)
+            m_ref[rows, :] = jnp.broadcast_to(jnp.max(top, axis=1, keepdims=True) * scale, top.shape)
 
     def stat_rows(stat):
         high = stat.astype(BF16).astype(F32)
@@ -184,21 +194,23 @@
         safe = jnp.where(live, weight, 1.0)
         return (jnp.where(live, total / safe, 0.0), jnp.where(live, top + jnp.log2(safe), CLOSED))
 
-    def weigh_tile(b, q, s_ref, m_ref):
-        top = m_ref[...]
-        total = None
-        for k in range(0, span, CHUNK):
-            parts = []
-            for x in range(k, k + CHUNK, 128):
-                parts.append(jnp.exp2(s_ref[:, x : x + 128] * scale - top).astype(BF16))
-            d = contract(jnp.concatenate(parts, axis=1), vaug[b, k : k + CHUNK, :], 1, 0)
-            total = d if total is None else total + d
-        mean, level = finish(total[:, 0:128], total[:, 128:256], top)
-        mean = mean.astype(BF16)
-        for g in range(4):
-            rows = slice(g * ROWS, (g + 1) * ROWS)
-            oloc[b, q, g // 2, g % 2, 0:ROWS, :] = mean[rows]
-            oloc[b, q, g // 2, g % 2, ROWS : ROWS + TAIL, :] = stat_rows(to_row(level[rows]))
+    def weigh_step(pairs, s_ref, m_ref):
+        for b, members, rows in by_rollout(pairs):
+            top = m_ref[rows, :]
+            total = None
+            for k in range(0, span, CHUNK):
+                parts = []
+                for x in range(k, k + CHUNK, 128):
+                    parts.append(jnp.exp2(s_ref[rows, x : x + 128] * scale - top).astype(BF16))
+                d = contract(jnp.concatenate(parts, axis=1), vaug[b, k : k + CHUNK, :], 1, 0)
+                total = d if total is None else total + d
+            mean, level = finish(total[:, 0:128], total[:, 128:256], top)
+            mean = mean.astype(BF16)
+            for i, p in enumerate(members):
+                for core in range(2):
+                    at_rows = slice((2 * i + core) * ROWS, (2 * i + core + 1) * ROWS)
+                    oloc[b, p, core, 0:ROWS, :] = mean[at_rows]
+                    oloc[b, p, core, ROWS : ROWS + TAIL, :] = stat_rows(to_row(level[at_rows]))
 
     def blend(pieces, levels):
         top = functools.reduce(jnp.maximum, levels)
@@ -209,14 +221,13 @@
         mixed = contract(left, jnp.concatenate(pieces, axis=0), 1, 0)
         return mixed, top + jnp.log2(total)
 
-    def chip_blend(b, q):
-        for g, pair in enumerate(TILES[q]):
-            mixed, level = blend(
-                [oloc[b, q, g, 0, 0:ROWS, :], r1[b, q, g, 0:ROWS, :]],
-                [stat_of(oloc[b, q, g, 0, ROWS : ROWS + TAIL, :]), stat_of(r1[b, q, g, ROWS : ROWS + TAIL, :])],
-            )
-            cp[b, pair, 0:ROWS, :] = mixed.astype(BF16)
-            cp[b, pair, ROWS : ROWS + TAIL, :] = stat_rows(level)
+    def chip_blend(b, p):
+        mixed, level = blend(
+            [oloc[b, p, 0, 0:ROWS, :], r1[b, p, 0:ROWS, :]],
+            [stat_of(oloc[b, p, 0, ROWS : ROWS + TAIL, :]), stat_of(r1[b, p, ROWS : ROWS + TAIL, :])],
+        )
+        cp[b, p, 0:ROWS, :] = mixed.astype(BF16)
+        cp[b, p, ROWS : ROWS + TAIL, :] = stat_rows(level)
 
     def new_part(b):
         blocks = [kvg[j, b].astype(F32) for j in range(slots)]
@@ -239,22 +250,28 @@
 
     def last_blend(b):
         sources = [cp.at[b, 0]] + [r2.at[b, p] for p in range(1, slots // 2)]
+        if b == rollouts - 1:
+            sources += [rx.at[i] for i in range(len(LAST))]
         pieces = [x[0:ROWS, :] for x in sources] + [onew[b]]
         levels = [stat_of(x[ROWS : ROWS + TAIL, :]) for x in sources] + [lnew[b, 0:1, :]]
         mixed, _ = blend(pieces, levels)
         token = c * tps + lax.div(lax.broadcasted_iota(jnp.int32, (ROWS, 128), 0), group)
         fin[b] = jnp.where(token < nlen_ref[b], mixed, 0.0).astype(BF16)
 
-    def send_r1(b, q):
-        remote(oloc.at[b, q, :, 1], r1.at[b, q], r1_send.at[b], r1_recv.at[b, q], partner, t)
-
-    def wait_r1(b, q):
-        await_bytes(r1.at[b, q], r1_recv.at[b, q])
-
-    def send_r2(b, q):
-        for p in TILES[q]:
-            if p:
-                remote(cp.at[b, p], r2.at[b, p], r2_send.at[b], r2_recv.at[b], ctx_peer[2 * p], t)
+    def send_r1(b, p):
+        remote(oloc.at[b, p, 1], r1.at[b, p], r1_send.at[b], r1_recv.at[b, p], partner, t)
+
+    def wait_r1(b, p):
+        await_bytes(r1.at[b, p], r1_recv.at[b, p])
+
+    def send_r2(b, p):
+        if p:
+            remote(cp.at[b, p], r2.at[b, p], r2_send.at[b], r2_recv.at[b], ctx_peer[2 * p], t)
+
+    def send_last(b):
+        for i, p in enumerate(LAST):
+            remote(oloc.at[b, p, 0], r2.at[b, p], r2_send.at[b], r2_recv.at[b], ctx_peer[2 * p], t)
+            remote(oloc.at[b, p, 1], rx.at[i], rx_send, rx_recv, ctx_peer[2 * p + 1], t)
 
     def wait_r2(b):
         await_bytes(r2.at[b, pl.ds(1, slots // 2 - 1)], r2_recv.at[b])
@@ -268,15 +285,13 @@
         v_copies[b].wait()
         prepare(b)
     own_copy.wait()
-    wait_a(0)
-    send_b(0)
-    wait_a(1)
-    send_b(1)
-    pass_on(0, 0)
-    pass_on(0, 1)
-    wait_odd(0, 0)
+    for b in range(rollouts):
+        wait_a(b)
+        send_b(b, 1)
+    send_b(0, *NEAR)
     bufs = ((s0, m0), (s1, m1))
-    score_tile(0, tile_queries(0, 0), *bufs[0])
+    wait_odd(*ORDER[0])
+    score_step(ORDER[0], *bufs[0])
 
     def kv_start():
         await_bytes(kva.at[pl.ds(0, tps - 1)], kv_recv)
@@ -286,17 +301,13 @@
                 asm[b, i : i + 1, :] = block[b : b + 1, :]
                 asm[b, tps + i : tps + i + 1, :] = block[rollouts + b : rollouts + b + 1, :]
         kvg[0] = asm[...].astype(BF16)
-        for j in GREETED:
+        for j in NEAR + FAR + (1,):
             remote(kvg.at[0], kvg.at[j], g_send, g_recv.at[j], ctx_peer[j], t)
 
     def kv_end():
         for j in range(1, slots, 2):
             await_bytes(kvg.at[j], g_recv.at[j])
 
-    def begin(b):
-        wait_a(b)
-        send_b(b)
-
     def finish_rollout(b):
         last_blend(b)
         send_r3(b)
@@ -307,52 +318,65 @@
     def at(when, step, what, *args):
         when[step].append((what, args))
 
-    at(before, 0, begin, 2)
-    at(before, 1, kv_start)
-    at(before, 3, begin, 3)
-    at(before, 7, kv_pass_on)
-    at(before, 9, kv_end)
-    for n, (b, q) in enumerate(ORDER):
-        if n >= 2:
-            at(before, n - 2, pass_on, b, q)
-    for n, (b, q) in enumerate(ORDER):
-        if n >= 1:
-            at(before, n - 1, wait_odd, b, q)
-        at(after, n, send_r1, b, q)
-        at(before, n + 2, wait_r1, b, q)
-        at(beside, n + 2, chip_blend, b, q)
-        at(after, n + 2, send_r2, b, q)
-    for b in range(rollouts):
-        at(beside, 9 + b, new_part, b)
+    at(before, 0, send_b, 0, *FAR)
+    at(before, 1, pass_on, (0, 1), (0, 3), (0, 4))
+    at(before, 1, send_b, 1, *NEAR, *FAR)
+    at(before, 2, pass_on, (0, 2))
+    at(before, 3, pass_on, (0, 5), (0, 6), (0, 7), (1, 1))
+    at(before, 4, pass_on, (1, 3), (1, 4))
+    at(before, 5, pass_on, (1, 2), (1, 5))
+    at(before, 6, pass_on, (1, 6), (1, 7))
+    for n in range(7, count - 2):
+        at(before, n, pass_on, *ORDER[n + 2])
+    for n in range(count - 1):
+        at(before, n, wait_odd, *ORDER[n + 1])
+    at(before, 2, kv_start)
+    at(before, 3, send_b, 2, *NEAR, *FAR)
+    at(before, 6, send_b, 3, *NEAR, *FAR)
+    at(before, 8, kv_pass_on)
+    at(before, 10, kv_end)
+    for n, pairs in enumerate(ORDER[:-1]):
+        for pair in pairs:
+            at(after, n, send_r1, *pair)
+    for n, pairs in enumerate(ORDER[:-1]):
+        later = min(n + 2, count)
+        for pair in pairs:
+            at(before, later, wait_r1, *pair)
+            at(beside, later, chip_blend, *pair)
+            at(after, later, send_r2, *pair)
+    at(after, count - 1, send_last, rollouts - 1)
+    for b in range(rollouts):
+        at(beside, 10 + b, new_part, b)
     for b, step in ((0, 12), (1, 14)):
         at(before, step, wait_r2, b)
         at(beside, step, last_blend, b)
         at(after, step, send_r3, b)
 
-    for n, (b, q) in enumerate(ORDER):
+    for n, pairs in enumerate(ORDER):
         for what, args in before[n]:
             what(*args)
-        if n + 1 < len(ORDER):
-            nb, nq = ORDER[n + 1]
-            score_tile(nb, tile_queries(nb, nq), *bufs[(n + 1) % 2])
-        weigh_tile(b, q, *bufs[n % 2])
+        if n + 1 < count:
+            score_step(ORDER[n + 1], *bufs[(n + 1) % 2])
+        weigh_step(pairs, *bufs[n % 2])
         for what, args in beside[n] + after[n]:
             what(*args)
-    for end in (count, count + 1):
-        for what, args in before[end] + beside[end] + after[end]:
-            what(*args)
-    for b in (2, 3):
-        wait_r2(b)
-        finish_rollout(b)
+    for what, args in before[count] + beside[count] + after[count]:
+        what(*args)
+    wait_r2(2)
+    finish_rollout(2)
+    wait_r2(3)
+    await_bytes(rx, rx_recv)
+    finish_rollout(3)
     keep = pltpu.make_async_copy(fin.at[:, my_rows, :], out_ref.at[:, my_rows, :], r3_own)
     keep.start()
 
     for b in range(rollouts):
         await_bytes(qall.at[b, 0, pl.ds(0, ROWS - group), :], a_send.at[b])
         await_bytes(qall.at[b, pl.ds(0, slots - 1)], b_send.at[b])
-        await_bytes(r1.at[b], r1_send.at[b])
+        await_bytes(r1.at[b, pl.ds(0, slots // 2 - (len(LAST) if b == rollouts - 1 else 0))], r1_send.at[b])
         await_bytes(r2.at[b, pl.ds(1, slots // 2 - 1)], r2_send.at[b])
     await_bytes(kva.at[pl.ds(0, tps - 1)], kv_send)
+    await_bytes(rx, rx_send)
     await_bytes(kvg.at[pl.ds(0, slots - 1)], g_send)
     await_bytes(fin.at[:, pl.ds(0, ROWS - group), :], r3_send)
     await_bytes(fin.at[:, pl.ds(0, ROWS - group), :], r3_recv)
@@ -362,7 +386,6 @@
 def shards(queries, new_keys, turn_value_rows, cache_keys, cache_values, cached_len, new_len, fold):
     rollouts, span = cache_keys.shape[0], cache_keys.shape[1]
     slots, tps = lax.axis_size("ctx"), lax.axis_size("tp")
-    tiles = slots // 4
     any_space = pl.BlockSpec(memory_space=pl.ANY)
     dma = pltpu.SemaphoreType.DMA
     block = (ROWS + TAIL, 128)
@@ -379,10 +402,11 @@
             pltpu.VMEM((4 * ROWS, span), F32),
             pltpu.VMEM((4 * ROWS, 128), F32),
             pltpu.VMEM((4 * ROWS, 128), F32),
-            pltpu.VMEM((rollouts, tiles, 2, 2) + block, BF16),
-            pltpu.VMEM((rollouts, tiles, 2) + block, BF16),
+            pltpu.VMEM((rollouts, slots // 2, 2) + block, BF16),
             pltpu.VMEM((rollouts, slots // 2) + block, BF16),
             pltpu.VMEM((rollouts, slots // 2) + block, BF16),
+            pltpu.VMEM((rollouts, slots // 2) + block, BF16),
+            pltpu.VMEM((len(LAST),) + block, BF16),
             pltpu.VMEM((rollouts, ROWS, 128), BF16),
             pltpu.VMEM((rollouts, ROWS, 128), BF16),
             pltpu.VMEM((rollouts, 8, 128), F32),
@@ -400,8 +424,9 @@
             dma, dma,
             dma((rollouts,)), dma((rollouts, slots)),
             dma, dma((slots,)),
-            dma((rollouts,)), dma((rollouts, tiles)),
+            dma((rollouts,)), dma((rollouts, slots // 2)),
             dma((rollouts,)), dma((rollouts,)),
+            dma, dma,
             dma, dma, dma,
         ],
         compiler_params=pltpu.CompilerParams(

time: 61.2 us -> 60.3 us (0.985)
  Pallas kernels: 59.3 us -> 58.6 us
    pallas_call x1, Pallas kernels: 59.3 us -> 58.6 us  [shards(): pl.pallas_call(kernel, out_shape=jax.ShapeDtypeStruct((rollouts, 128, 128...]
where the time goes in v1:
time: 60.3 us; the launch traced here: 60.2 us
  Pallas kernels  58.6 us (97%)
  local copies, waits for them, and re-layouts  1.57 us (3%)
    pallas_call x1, Pallas kernels, shards(): pl.pallas_call(kernel, out_shape=jax.ShapeDtypeStruct((rollouts, 128, 128...  58.6 us
    unnamed x1, local copies, waits for them, and re-layouts  1.57 us

profile of v1, /device:TPU:0, one launch (start us, length us, event | category | flops | bytes accessed | tf_op | source)
XLA Modules:
  0.0 60.2 jit_solution(11562001250762988957)
XLA Ops:
  0.0 58.6 %turn_attention.1 = bf16[4,128,128]{2,1,0:T(8,128)(2,1)} custom-call(bf16[4,128,128]{2,1,0:T(8,128)(2,1)} %bitcast.11, bf16[4,8,128]{2,1,0:T(8,128)(2,1)} %bitcast.12, bf16[4,8,128]{2,1,0:T(8,128)(2,1)} %bitcast.13, bf16[4,2048,128]{2,1,0:T(8,128)(2,1)} %bitcast.8, bf16[4,2048,128]{2,1,0:T(8,128)(2,1)} %bitcast.9, s32[4]{0:T(128)} %clen_hbm.1, s32[4]{0:T(128)} %nlen_hbm.1, ...), custom_call_target="tpu_custom_call" | custom-call | tf_op jit(solution)/shard_map/turn_attention/pallas_call | solution.py:392
  58.6 1.6 %copy.11 = bf16[4,1,128,128]{3,2,1,0:T(8,128)(2,1)} copy(bf16[4,1,128,128]{3,2,1,0:T(8,128)(2,1)} %bitcast.10) | data formatting | bytes 262144

commit v2 on v1

--- a/solution.py
+++ b/solution.py
@@ -17,14 +17,14 @@
 CHUNK = 512
 NEAR = (2, 6, 8, 4)
 FAR = (10, 14, 12)
-LAST = (3, 1)
+LAST = (3, 1, 6, 5)
 GREETED = NEAR + FAR + (1,) + tuple(2 * p + 1 for p in LAST)
 ORDER = (
     ((0, 0), (1, 0)), ((2, 0), (3, 0)),
     ((0, 1), (0, 3)), ((0, 4), (0, 2)), ((0, 5), (0, 6)), ((0, 7), (1, 1)),
     ((1, 3), (1, 4)), ((1, 2), (1, 5)), ((1, 6), (1, 7)),
     ((2, 7), (2, 6)), ((2, 5), (2, 2)), ((2, 4), (2, 3)), ((2, 1), (3, 7)),
-    ((3, 6), (3, 5)), ((3, 2), (3, 4)), ((3, 3), (3, 1)),
+    ((3, 2), (3, 4)), ((3, 6), (3, 5)), ((3, 3), (3, 1)),
 )
 
 
@@ -268,8 +268,9 @@
         if p:
             remote(cp.at[b, p], r2.at[b, p], r2_send.at[b], r2_recv.at[b], ctx_peer[2 * p], t)
 
-    def send_last(b):
-        for i, p in enumerate(LAST):
+    def send_last(pairs):
+        for b, p in pairs:
+            i = LAST.index(p)
             remote(oloc.at[b, p, 0], r2.at[b, p], r2_send.at[b], r2_recv.at[b], ctx_peer[2 * p], t)
             remote(oloc.at[b, p, 1], rx.at[i], rx_send, rx_recv, ctx_peer[2 * p + 1], t)
 
@@ -335,16 +336,17 @@
     at(before, 6, send_b, 3, *NEAR, *FAR)
     at(before, 8, kv_pass_on)
     at(before, 10, kv_end)
-    for n, pairs in enumerate(ORDER[:-1]):
+    for n, pairs in enumerate(ORDER[:-2]):
         for pair in pairs:
             at(after, n, send_r1, *pair)
-    for n, pairs in enumerate(ORDER[:-1]):
+    for n, pairs in enumerate(ORDER[:-2]):
         later = min(n + 2, count)
         for pair in pairs:
             at(before, later, wait_r1, *pair)
             at(beside, later, chip_blend, *pair)
             at(after, later, send_r2, *pair)
-    at(after, count - 1, send_last, rollouts - 1)
+    for n in (count - 2, count - 1):
+        at(after, n, send_last, ORDER[n])
     for b in range(rollouts):
         at(beside, 10 + b, new_part, b)
     for b, step in ((0, 12), (1, 14)):

time: 60.3 us -> 61.6 us (1.022)
  Pallas kernels: 58.6 us -> 59.5 us
    pallas_call x1, Pallas kernels: 58.6 us -> 59.5 us  [shards(): pl.pallas_call(kernel, out_shape=jax.ShapeDtypeStruct((rollouts, 128, 128...]
where the time goes in v2:
time: 61.6 us; the launch traced here: 61 us
  Pallas kernels  59.5 us (97%)
  local copies, waits for them, and re-layouts  1.57 us (3%)
    pallas_call x1, Pallas kernels, shards(): pl.pallas_call(kernel, out_shape=jax.ShapeDtypeStruct((rollouts, 128, 128...  59.5 us
    unnamed x1, local copies, waits for them, and re-layouts  1.57 us

profile of v2, /device:TPU:0, one launch (start us, length us, event | category | flops | bytes accessed | tf_op | source)
XLA Modules:
  0.0 61.0 jit_solution(9387388383628228329)
XLA Ops:
  0.0 59.5 %turn_attention.1 = bf16[4,128,128]{2,1,0:T(8,128)(2,1)} custom-call(bf16[4,128,128]{2,1,0:T(8,128)(2,1)} %bitcast.11, bf16[4,8,128]{2,1,0:T(8,128)(2,1)} %bitcast.12, bf16[4,8,128]{2,1,0:T(8,128)(2,1)} %bitcast.13, bf16[4,2048,128]{2,1,0:T(8,128)(2,1)} %bitcast.8, bf16[4,2048,128]{2,1,0:T(8,128)(2,1)} %bitcast.9, s32[4]{0:T(128)} %clen_hbm.1, s32[4]{0:T(128)} %nlen_hbm.1, ...), custom_call_target="tpu_custom_call" | custom-call | tf_op jit(solution)/shard_map/turn_attention/pallas_call | solution.py:394
  59.5 1.6 %copy.11 = bf16[4,1,128,128]{3,2,1,0:T(8,128)(2,1)} copy(bf16[4,1,128,128]{3,2,1,0:T(8,128)(2,1)} %bitcast.10) | data formatting | bytes 262144
